TPU v7x, 768 devices: a whole 4x8x12 slice. The times are simulated.
768 devices in a mesh: dp: 96 (over x, z, core), section: 8 (over y).
Axes of the slice: x: 4, y: 8, z: 12, core: 2. Of those that a mesh axis runs over, the one named last changes fastest.
Arguments:
- grads: bfloat16 [96, 2, 8, 6144, 128], P('dp', None, 'section'), may hold values from -3.5 to 3.5
- params: float32 [8, 6144, 128], P('section', 'dp'), may hold values from -4 to 4
- first_moment: float32 [8, 6144, 128], P('section', 'dp'), may hold values from -1.5 to 1.5
- second_moment: float32 [8, 6144, 128], P('section', 'dp'), may hold values from 0.01 to 0.2
- owners: int32 [96, 8, 8], P('dp', 'section'), may hold values from 0 to 7, as said below
Outputs:
- ckpt_param: float32 [96, 2048, 128], P('dp', 'section')
- ckpt_first: float32 [96, 2048, 128], P('dp', 'section')
- ckpt_second: float32 [96, 2048, 128], P('dp', 'section')
Inputs may be any that keep to these rules, and one draw needn't show every extreme that they name: `owners`: each device names a writer for each of its 8 pieces and names no writer more than 4 times; in each group of devices sharing a dp index, one writer is named exactly 4 times by every device of the group.
All inputs are finite; a program needn't handle non-finite values.
Results may differ from a plain program's by a relative error of at most 0.0003.
Values sent between devices are 32-bit elements; how exact they have to be, the bound alone decides.
No kernel may reach another device: no remote copies, remote signals or barrier semaphores. Data moves between devices by JAX's collectives and lax.ppermute only.
A program may use at most 32 MiB of HBM per device.

v0:
```python
import jax
import jax.numpy as jnp
from jax import lax
from jax.sharding import PartitionSpec as P

beta_one = 0.9
beta_two = 0.95
learn_rate = 0.03
decay_rate = 0.1
epsilon = 1e-08


def body(grads, params, first_moment, second_moment, owners):
    partial_value = grads[0, :, 0]
    shard_rows = params.shape[1]
    lane_count = params.shape[2]
    local_total = jnp.sum(partial_value, axis=0, dtype=jnp.float32)
    gradient = lax.psum_scatter(local_total, "dp", scatter_dimension=0, tiled=True)
    weights = params[0]
    momentum = beta_one * first_moment[0] + (1.0 - beta_one) * gradient
    variance = beta_two * second_moment[0] + (1.0 - beta_two) * gradient * gradient
    updated = weights - learn_rate * (
        momentum / (jnp.sqrt(variance) + epsilon) + decay_rate * weights
    )
    owner_list = owners[0, 0]
    pieces = owner_list.shape[0]
    piece_rows = shard_rows // pieces
    capacity = pieces // 2
    writers = lax.axis_size("section")
    slot_count = writers * capacity
    states = jnp.stack([updated, momentum, variance]).reshape(3, pieces, piece_rows, lane_count)
    slot_index = jnp.arange(slot_count, dtype=jnp.int32)
    highest = lax.Precision.HIGHEST
    everyone, everyone_owner = (
        lax.all_gather(states[None], "section", axis=0, tiled=True),
        lax.all_gather(owner_list.astype(jnp.float32)[None], "section", axis=0, tiled=True),
    )
    owned_here = (everyone_owner.astype(jnp.int32) == lax.axis_index("section")).astype(jnp.int32)
    source_counts = jnp.sum(owned_here, axis=1)
    starts = jnp.cumsum(source_counts) - source_counts
    target = starts[:, None] + jnp.cumsum(owned_here, axis=1) - owned_here
    placing = ((target[:, :, None] == slot_index) & (owned_here[:, :, None] == 1)).astype(
        jnp.float32
    )
    packed = jnp.einsum("spo,saprl->aorl", placing, everyone, precision=highest)
    packed = packed.reshape(3, 1, slot_count * piece_rows, lane_count)
    return (packed[0], packed[1], packed[2])


def solution(mesh):
    in_specs = (
        P("dp", None, "section", None, None),
        P("section", "dp", None),
        P("section", "dp", None),
        P("section", "dp", None),
        P("dp", "section", None),
    )
    out_specs = (P("dp", "section", None), P("dp", "section", None), P("dp", "section", None))
    return jax.shard_map(body, mesh=mesh, in_specs=in_specs, out_specs=out_specs, check_vma=False)
```

profile of v0, /device:TPU:6, one launch (start us, length us, event | category | flops | bytes accessed | tf_op | source)
XLA Modules:
  0.0 268.7 jit_solution(16650428538954603057)
XLA Ops:
  7.2 0.0 reduce-scatter.2.cloned.1.call-start
  7.2 4.4 %convert_reduce_fusion = f32[6144,128]{1,0:T(8,128)} fusion(bf16[1,2,1,6144,128]{4,3,2,1,0:T(8,128)(2,1)} %param.5), kind=kLoop, calls=%fused_computation | loop fusion | flops 2359296 | bytes 6291456 | tf_op jit(solution)/shard_map/reduce_sum | solution.py:17
  11.7 0.0 copy-start.3
  11.7 0.0 copy-start
  11.7 0.0 copy-start.1
  11.7 0.0 copy-start.2
  11.7 0.0 reduce-scatter.2.cloned.1.call-update
  11.7 0.6 copy-done.3
  12.3 16.6 %all-gather = f32[8,1,8]{2,1,0:T(1,128)S(1)} all-gather(f32[1,1,8]{2,1,0:T(1,128)S(1)} %convert_element_type.25), channel_id=2, replica_groups=mesh['dp'=96,'section'=8] {'section'}, dimensions={0}, use_global_device_ids=true | all-gather | bytes 288 | tf_op jit(solution)/shard_map/all_gather | solution.py:36
  29.0 0.2 reduce_window_sum.18
  29.1 0.1 convert_reduce_fusion.1
  29.2 0.2 reduce-window.8
  29.4 0.1 add_subtract_fusion
  29.5 0.1 copy.21
  29.6 0.1 copy.22
  29.7 201.8 %reduce-scatter.2.cloned.1.call-done = f32[64,128]{1,0:T(8,128)} async-done(((f32[6144,128]{1,0:T(8,128)}), f32[64,128]{1,0:T(8,128)}) %reduce-scatter.2.cloned.1.call-update) | async-done | bytes 32784 | tf_op jit(solution)/shard_map/reduce_scatter | solution.py:18
  231.4 0.0 copy-done
  231.4 0.0 copy-done.1
  231.4 0.0 copy-done.2
  231.4 0.8 fusion.4
  232.2 27.1 %all_gather.6 = f32[8,3,8,8,128]{4,3,2,1,0:T(8,128)S(1)} all-gather(f32[1,3,8,8,128]{4,3,2,1,0:T(8,128)S(1)} %pad_maximum_fusion), channel_id=1, replica_groups=mesh['dp'=96,'section'=8] {'section'}, dimensions={0}, use_global_device_ids=true | all-gather | bytes 884736 | tf_op jit(solution)/shard_map/all_gather | solution.py:35
  259.3 0.9 convolution_bitcast_fusion
  260.2 0.7 copy.34
  261.0 0.9 copy_bitcast_fusion
  (6 shorter events, 0.1 us)
Async XLA Ops:
  7.2 224.3 %reduce-scatter.2.cloned.1.call-start = ((), (), s32[]{:S(2)}) async-start(), calls=%async_computation.1 | async-start | bytes 3178496 | tf_op jit(solution)/shard_map/reduce_scatter | solution.py:18
  11.7 0.7 copy-start.3
  11.7 219.8 %copy-start = (f32[1,64,128]{2,1,0:T(8,128)S(1)}, f32[1,64,128]{2,1,0:T(8,128)}, u32[]{:S(2)}) copy-start(f32[1,64,128]{2,1,0:T(8,128)} %param.6) | copy-start | bytes 98308
  11.7 219.8 %copy-start.1 = (f32[1,64,128]{2,1,0:T(8,128)S(1)}, f32[1,64,128]{2,1,0:T(8,128)}, u32[]{:S(2)}) copy-start(f32[1,64,128]{2,1,0:T(8,128)} %param.7) | copy-start | bytes 98308
  11.7 219.8 %copy-start.2 = (f32[1,64,128]{2,1,0:T(8,128)S(1)}, f32[1,64,128]{2,1,0:T(8,128)}, u32[]{:S(2)}) copy-start(f32[1,64,128]{2,1,0:T(8,128)} %param.8) | copy-start | bytes 98308
Sparse Core Ops, SparseCore 0:
  13.3 218.1 reduce-scatter.1
where the time goes:
time: 270 us; the launch traced here: 269 us
  waiting for transfers between devices  202 us (75%)
  blocking collectives  43.7 us (16%)
  between operations  14.1 us (5%)
  other arithmetic  5.8 us (2%)
    reduce_scatter x1, waiting for transfers between devices, body(): lax.psum_scatter(local_total, 'dp', scatter_dimension=0, tiled=True)  202 us
    all_gather x1, blocking collectives, body(): lax.all_gather(states[None], 'section', axis=0, tiled=True)  27.1 us
    all_gather x1, blocking collectives, body(): lax.all_gather(owner_list.astype(jnp.float32)[None], 'section', axis=0, t...  16.6 us
  transfers between devices with their start and end apart: 1, of which 1 were waited for; matrix products, arithmetic and copies ran while one was open for 0% of the time, Pallas kernels for 0%

commit v1 on v0

v1 whole, which is shorter than its diff:
```python
import jax
import jax.numpy as jnp
from jax import lax
from jax.experimental import pallas as pl
from jax.experimental.pallas import tpu as pltpu
from jax.sharding import PartitionSpec as P

beta_one = 0.9
beta_two = 0.95
learn_rate = 0.03
decay_rate = 0.1
epsilon = 1e-08

LANE = 128
X, Z, CORE = 4, 12, 2
PAIR = 2
FAR = Z // PAIR
ROWS = 64
PIECES, PIECE = 8, 8
WRITERS, CAP = 8, 4
STATE = 3 * CAP * PIECE
BLOCK = STATE + PIECE


def device_of(x, z, core):
    return (x * Z + z) * CORE + core


def near_groups():
    return [
        [device_of(x, PAIR * a + b, c) for x in range(X) for b in range(PAIR)]
        for a in range(FAR)
        for c in range(CORE)
    ]


def far_groups():
    return [
        [device_of(x, PAIR * a + b, c) for a in range(FAR)]
        for x in range(X)
        for b in range(PAIR)
        for c in range(CORE)
    ]


def send_kernel(core_ref, grads_ref, out_ref):
    for a in range(FAR):
        for b in range(PAIR):
            first = grads_ref[0, 0, a, b, 0].astype(jnp.float32)
            out_ref[0, b, a] = first + grads_ref[1, 0, a, b, 0].astype(jnp.float32)


def join_kernel(core_ref, grads_ref, got_ref, out_ref):
    for a in range(FAR):
        for b in range(PAIR):
            first = grads_ref[0, 0, a, b, 0].astype(jnp.float32)
            own = first + grads_ref[1, 0, a, b, 0].astype(jnp.float32)
            out_ref[0, b, a] = own + got_ref[0, b, a]


def half_call(kernel, core, grads, *got):
    block = (1, PAIR, FAR, ROWS, LANE)
    stream = pl.BlockSpec(block, lambda i, core_ref: (i, 0, 0, 0, 0))
    return pl.pallas_call(
        kernel,
        out_shape=jax.ShapeDtypeStruct((X, PAIR, FAR, ROWS, LANE), jnp.float32),
        grid_spec=pltpu.PrefetchScalarGridSpec(
            num_scalar_prefetch=1,
            grid=(X,),
            in_specs=[
                pl.BlockSpec(
                    (2, 1, FAR, PAIR, 1, ROWS, LANE),
                    lambda i, core_ref: (0, i, 0, 0, core_ref[0], 0, 0),
                )
            ]
            + [stream] * len(got),
            out_specs=stream,
        ),
        cost_estimate=pl.CostEstimate(
            flops=2 * X * Z * ROWS * LANE,
            bytes_accessed=(8 + 4 * len(got)) * X * Z * ROWS * LANE,
            transcendentals=0,
        ),
    )(core, grads, *got)


def pack_kernel(owner_ref, parts_ref, params_ref, first_ref, second_ref, out_ref):
    gradient = parts_ref[0]
    for a in range(1, FAR):
        gradient = gradient + parts_ref[a]
    weights = params_ref[...]
    momentum = beta_one * first_ref[...] + (1.0 - beta_one) * gradient
    variance = beta_two * second_ref[...] + (1.0 - beta_two) * gradient * gradient
    updated = weights - learn_rate * (
        momentum / (jnp.sqrt(variance) + epsilon) + decay_rate * weights
    )
    owners = [owner_ref[p] for p in range(PIECES)]
    out_ref[...] = jnp.zeros_like(out_ref)
    for w in range(WRITERS):
        count = sum((owner == w).astype(jnp.int32) for owner in owners)
        out_ref[w, STATE:BLOCK] = jnp.full((PIECE, LANE), count.astype(jnp.float32))
    for p in range(PIECES):
        slot = jnp.int32(0)
        for q in range(p):
            slot = slot + (owners[q] == owners[p]).astype(jnp.int32)
        rows = slice(p * PIECE, (p + 1) * PIECE)
        for k, state in enumerate((updated, momentum, variance)):
            at = pl.multiple_of((slot + k * CAP) * PIECE, PIECE)
            out_ref[owners[p], pl.ds(at, PIECE)] = state[rows]


def place_kernel(got_ref, param_ref, first_ref, second_ref):
    outs = (param_ref, first_ref, second_ref)
    for out_ref in outs:
        out_ref[...] = jnp.zeros_like(out_ref)
    start = jnp.int32(0)
    for s in range(WRITERS):
        at = pl.multiple_of(start * PIECE, PIECE)
        for k, out_ref in enumerate(outs):
            rows = slice(k * CAP * PIECE, (k + 1) * CAP * PIECE)
            out_ref[0, pl.ds(at, CAP * PIECE)] = got_ref[s, rows]
        if s < WRITERS - 1:
            start = start + jnp.max(got_ref[s, STATE:BLOCK]).astype(jnp.int32)


def body(grads, params, first_moment, second_moment, owners):
    vmem = pl.BlockSpec(memory_space=pltpu.VMEM)
    smem = pl.BlockSpec(memory_space=pltpu.SMEM)
    core = lax.rem(lax.axis_index("dp"), CORE).astype(jnp.int32).reshape(1)
    grads = grads.reshape(2, X, FAR, PAIR, CORE, ROWS, LANE)
    sent = half_call(send_kernel, 1 - core, grads)
    swap = [(i, i ^ 1) for i in range(X * Z * CORE)]
    got = lax.ppermute(sent, "dp", swap)
    chip = half_call(join_kernel, core, grads, got)
    near = lax.all_to_all(
        chip.reshape(X * PAIR, FAR * ROWS, LANE), "dp", 0, 0, axis_index_groups=near_groups()
    )
    near = jnp.sum(near, axis=0).reshape(FAR, ROWS, LANE)
    far = lax.all_to_all(near, "dp", 0, 0, axis_index_groups=far_groups())
    packed = pl.pallas_call(
        pack_kernel,
        out_shape=jax.ShapeDtypeStruct((WRITERS, BLOCK, LANE), jnp.float32),
        in_specs=[smem] + [vmem] * 4,
        out_specs=vmem,
    )(owners.reshape(PIECES), far, params[0], first_moment[0], second_moment[0])
    handed = lax.all_to_all(packed, "section", 0, 0)
    out = jax.ShapeDtypeStruct((1, WRITERS * CAP * PIECE, LANE), jnp.float32)
    return pl.pallas_call(
        place_kernel,
        out_shape=(out,) * 3,
        in_specs=[vmem],
        out_specs=(vmem,) * 3,
    )(handed)


def solution(mesh):
    in_specs = (
        P("dp", None, "section", None, None),
        P("section", "dp", None),
        P("section", "dp", None),
        P("section", "dp", None),
        P("dp", "section", None),
    )
    out_specs = (P("dp", "section", None), P("dp", "section", None), P("dp", "section", None))
    return jax.shard_map(body, mesh=mesh, in_specs=in_specs, out_specs=out_specs, check_vma=False)
```

time: 270 us -> 91 us (0.34)
  waiting for transfers between devices: 202 us -> 3.59 us
  blocking collectives: 43.7 us -> 71.5 us
  between operations: 14.1 us -> 0.66 us
  Pallas kernels: 0 us -> 11.2 us
  other arithmetic: 5.8 us -> 0.09 us
    reduce_scatter x1 -> x0, waiting for transfers between devices: 202 us -> none  [body(): lax.psum_scatter(local_total, 'dp', scatter_dimension=0, tiled=True)]
    all_to_all x0 -> x3, blocking collectives: none -> 71.5 us  [the longest x1 32.5 us: body(): lax.all_to_all(chip.reshape(X * PAIR, FAR * ROWS, LANE), 'dp', 0, 0, axis...]
    all_gather x2 -> x0, blocking collectives: 43.7 us -> none  [the longest x1 27.1 us: body(): lax.all_gather(states[None], 'section', axis=0, tiled=True)]
    pallas_call x0 -> x4, Pallas kernels: none -> 11.2 us  [the longest x2 7.53 us: half_call(): pl.pallas_call(kernel, out_shape=jax.ShapeDtypeStruct((X, PAIR, FAR, ROWS...]
    reduce_sum x2 -> x1, other arithmetic: 4.56 us -> 0.09 us  [body(): near = jnp.sum(near, axis=0).reshape(FAR, ROWS, LANE)]
    ppermute x0 -> x1, waiting for transfers between devices: none -> 3.59 us  [body(): got = lax.ppermute(sent, 'dp', swap)]
where the time goes in v1:
time: 91 us; the launch traced here: 90.1 us
  blocking collectives  71.5 us (79%)
  Pallas kernels  11.2 us (12%)
  waiting for transfers between devices  3.59 us (4%)
  starting transfers between devices  1.91 us (2%)
  local copies, waits for them, and re-layouts  1.15 us (1%)
    all_to_all x1, blocking collectives, body(): lax.all_to_all(chip.reshape(X * PAIR, FAR * ROWS, LANE), 'dp', 0, 0, axis...  32.5 us
    all_to_all x1, blocking collectives, body(): far = lax.all_to_all(near, 'dp', 0, 0, axis_index_groups=far_groups())  19.5 us
    all_to_all x1, blocking collectives, body(): handed = lax.all_to_all(packed, 'section', 0, 0)  19.4 us
    pallas_call x2, Pallas kernels, half_call(): pl.pallas_call(kernel, out_shape=jax.ShapeDtypeStruct((X, PAIR, FAR, ROWS...  7.53 us
    ppermute x1, waiting for transfers between devices, body(): got = lax.ppermute(sent, 'dp', swap)  3.59 us
    ppermute x1, starting transfers between devices, body(): got = lax.ppermute(sent, 'dp', swap)  1.91 us
    pallas_call x1, Pallas kernels, body(): pl.pallas_call(place_kernel, out_shape=(out,) * 3, in_specs=[vmem], out_s...  1.89 us
    pallas_call x1, Pallas kernels, body(): pl.pallas_call(pack_kernel, out_shape=jax.ShapeDtypeStruct((WRITERS, BLOC...  1.83 us
  transfers between devices with their start and end apart: 1, of which 1 were waited for; matrix products, arithmetic and copies ran while one was open for 0% of the time, Pallas kernels for 0%

profile of v1, /device:TPU:6, one launch (start us, length us, event | category | flops | bytes accessed | tf_op | source)
XLA Modules:
  0.0 90.1 jit_solution(12176010218402512127)
XLA Ops:
  0.6 3.6 %shard_map.76 = f32[4,2,6,64,128]{4,3,2,1,0:T(8,128)} custom-call(s32[1]{0:T(128)S(6)} %sub.3.core_ref, bf16[2,4,6,2,2,64,128]{6,5,4,3,2,1,0:T(8,128)(2,1)} %bitcast.8), custom_call_target="tpu_custom_call" | custom-call | flops 786432 | bytes 3145728 | tf_op jit(solution)/shard_map/pallas_call | solution.py:64
  4.3 1.9 %collective-permute-start = (f32[4,2,6,64,128]{4,3,2,1,0:T(8,128)}, f32[4,2,6,64,128]{4,3,2,1,0:T(8,128)S(1)}, u32[]{:S(2)}, u32[]{:S(2)}) collective-permute-start(f32[4,2,6,64,128]{4,3,2,1,0:T(8,128)} %shard_map.76), channel_id=1, source_target_pairs={{0,8},{8,0},{16,24},{24,16},{32,40},{40,32},{48,56},{56,48},{64,72... | collective-permute-start | bytes 4718600 | tf_op jit(solution)/shard_map/ppermute | solution.py:133
  6.2 3.6 %collective-permute-done.got_ref = f32[4,2,6,64,128]{4,3,2,1,0:T(8,128)S(1)} collective-permute-done((f32[4,2,6,64,128]{4,3,2,1,0:T(8,128)}, f32[4,2,6,64,128]{4,3,2,1,0:T(8,128)S(1)}, u32[]{:S(2)}, u32[]{:S(2)}) %collective-permute-start) | collective-permute-done | bytes 1572896 | tf_op jit(solution)/shard_map/ppermute | solution.py:133
  9.8 0.0 copy-start
  9.8 1.2 %copy-done = f32[4,2,6,64,128]{4,3,2,1,0:T(8,128)} copy-done((f32[4,2,6,64,128]{4,3,2,1,0:T(8,128)}, f32[4,2,6,64,128]{4,3,2,1,0:T(8,128)S(1)}, u32[]{:S(2)}) %copy-start) | copy-done | bytes 1572888
  10.9 3.9 %shard_map.77 = f32[4,2,6,64,128]{4,3,2,1,0:T(8,128)} custom-call(s32[1]{0:T(128)} %bitcast.1.core_ref, bf16[2,4,6,2,2,64,128]{6,5,4,3,2,1,0:T(8,128)(2,1)} %bitcast.9, f32[4,2,6,64,128]{4,3,2,1,0:T(8,128)} %copy-done), custom_call_target="tpu_custom_call" | custom-call | flops 786432 | bytes 4718592 | tf_op jit(solution)/shard_map/pallas_call | solution.py:64
  14.8 32.5 %all_to_all.15 = f32[8,384,128]{2,1,0:T(8,128)S(1)} all-to-all(f32[8,384,128]{2,1,0:T(8,128)} %bitcast.10), channel_id=1, replica_groups={{0,16,192,208,384,400,576,592},{8,24,200,216,392,408,584,600},{32,48,22..., dimensions={0} | all-to-all | bytes 3145728 | tf_op jit(solution)/shard_map/all_to_all | solution.py:135
  47.3 0.1 reduce_sum.9
  47.4 19.5 %all_to_all.16.parts_ref = f32[6,64,128]{2,1,0:T(8,128)} all-to-all(f32[6,64,128]{2,1,0:T(8,128)S(1)} %bitcast.11), channel_id=1, replica_groups={{0,32,64,96,128,160},{8,40,72,104,136,168},{16,48,80,112,144,176},{24,5..., dimensions={0} | all-to-all | bytes 393216 | tf_op jit(solution)/shard_map/all_to_all | solution.py:139
  66.9 1.8 %shard_map.78 = f32[8,104,128]{2,1,0:T(8,128)} custom-call(s32[8]{0:T(128)} %bitcast.15, f32[6,64,128]{2,1,0:T(8,128)} %all_to_all.16.parts_ref, f32[64,128]{1,0:T(8,128)} %bitcast.12, f32[64,128]{1,0:T(8,128)} %bitcast.13, f32[64,128]{1,0:T(8,128)} %bitcast.14), custom_call_target="tpu_custom_call" | custom-call | tf_op jit(solution)/shard_map/pallas_call | solution.py:140
  68.8 19.4 %all_to_all.17.got_ref = f32[8,104,128]{2,1,0:T(8,128)} all-to-all(f32[8,104,128]{2,1,0:T(8,128)} %shard_map.78), channel_id=1, replica_groups=mesh['dp'=96,'section'=8] {'section'}, dimensions={0} | all-to-all | bytes 851968 | tf_op jit(solution)/shard_map/all_to_all | solution.py:146
  88.2 1.9 %shard_map.79 = (f32[1,256,128]{2,1,0:T(8,128)}, f32[1,256,128]{2,1,0:T(8,128)}, f32[1,256,128]{2,1,0:T(8,128)}) custom-call(f32[8,104,128]{2,1,0:T(8,128)} %all_to_all.17.got_ref), custom_call_target="tpu_custom_call" | custom-call | tf_op jit(solution)/shard_map/pallas_call | solution.py:148
Async XLA Ops:
  4.3 5.5 %collective-permute-start = (f32[4,2,6,64,128]{4,3,2,1,0:T(8,128)}, f32[4,2,6,64,128]{4,3,2,1,0:T(8,128)S(1)}, u32[]{:S(2)}, u32[]{:S(2)}) collective-permute-start(f32[4,2,6,64,128]{4,3,2,1,0:T(8,128)} %shard_map.76), channel_id=1, source_target_pairs={{0,8},{8,0},{16,24},{24,16},{32,40},{40,32},{48,56},{56,48},{64,72... | collective-permute-start | bytes 4718600 | tf_op jit(solution)/shard_map/ppermute | solution.py:133
  9.8 1.2 %copy-start = (f32[4,2,6,64,128]{4,3,2,1,0:T(8,128)}, f32[4,2,6,64,128]{4,3,2,1,0:T(8,128)S(1)}, u32[]{:S(2)}) copy-start(f32[4,2,6,64,128]{4,3,2,1,0:T(8,128)S(1)} %collective-permute-done.got_ref) | copy-start | bytes 4718596

commit v2 on v1

--- a/solution.py
+++ b/solution.py
@@ -76,6 +76,7 @@
             + [stream] * len(got),
             out_specs=stream,
         ),
+        compiler_params=pltpu.CompilerParams(vmem_limit_bytes=8 * 1024 * 1024),
         cost_estimate=pl.CostEstimate(
             flops=2 * X * Z * ROWS * LANE,
             bytes_accessed=(8 + 4 * len(got)) * X * Z * ROWS * LANE,
@@ -142,6 +143,7 @@
         out_shape=jax.ShapeDtypeStruct((WRITERS, BLOCK, LANE), jnp.float32),
         in_specs=[smem] + [vmem] * 4,
         out_specs=vmem,
+        compiler_params=pltpu.CompilerParams(vmem_limit_bytes=8 * 1024 * 1024),
     )(owners.reshape(PIECES), far, params[0], first_moment[0], second_moment[0])
     handed = lax.all_to_all(packed, "section", 0, 0)
     out = jax.ShapeDtypeStruct((1, WRITERS * CAP * PIECE, LANE), jnp.float32)
@@ -150,6 +152,7 @@
         out_shape=(out,) * 3,
         in_specs=[vmem],
         out_specs=(vmem,) * 3,
+        compiler_params=pltpu.CompilerParams(vmem_limit_bytes=8 * 1024 * 1024),
     )(handed)
 
 

time: 91 us -> 82 us (0.901)
  Pallas kernels: 11.2 us -> 2.32 us
    pallas_call x2, Pallas kernels: 7.53 us -> 0.77 us  [half_call(): pl.pallas_call(kernel, out_shape=jax.ShapeDtypeStruct((X, PAIR, FAR, ROWS...]
    pallas_call x1, Pallas kernels: 1.83 us -> 0.66 us  [body(): pl.pallas_call(pack_kernel, out_shape=jax.ShapeDtypeStruct((WRITERS, BLOC...]
    all_to_all x1, blocking collectives: 32.5 us -> 31.4 us  [body(): lax.all_to_all(chip.reshape(X * PAIR, FAR * ROWS, LANE), 'dp', 0, 0, axis...]
    pallas_call x1, Pallas kernels: 1.89 us -> 0.88 us  [body(): pl.pallas_call(place_kernel, out_shape=(out,) * 3, in_specs=[vmem], out_s...]
    unnamed x2 -> x12, local copies, waits for them, and re-layouts: 1.15 us -> 1.9 us
where the time goes in v2:
time: 82 us; the launch traced here: 81.3 us
  blocking collectives  70.9 us (86%)
  waiting for transfers between devices  3.38 us (4%)
  Pallas kernels  2.32 us (3%)
  starting transfers between devices  2.05 us (2%)
  local copies, waits for them, and re-layouts  1.9 us (2%)
    all_to_all x1, blocking collectives, body(): lax.all_to_all(chip.reshape(X * PAIR, FAR * ROWS, LANE), 'dp', 0, 0, axis...  31.4 us
    all_to_all x1, blocking collectives, body(): far = lax.all_to_all(near, 'dp', 0, 0, axis_index_groups=far_groups())  20.3 us
    all_to_all x1, blocking collectives, body(): handed = lax.all_to_all(packed, 'section', 0, 0)  19.1 us
    ppermute x1, waiting for transfers between devices, body(): got = lax.ppermute(sent, 'dp', swap)  3.38 us
    ppermute x1, starting transfers between devices, body(): got = lax.ppermute(sent, 'dp', swap)  2.05 us
    unnamed x12, local copies, waits for them, and re-layouts  1.9 us
  transfers between devices with their start and end apart: 1, of which 1 were waited for; matrix products, arithmetic and copies ran while one was open for 0% of the time, Pallas kernels for 0%

profile of v2, /device:TPU:6, one launch (start us, length us, event | category | flops | bytes accessed | tf_op | source)
XLA Modules:
  0.0 81.3 jit_solution(635824949796134131)
XLA Ops:
  0.6 0.0 copy-start
  0.7 1.9 %copy-done = bf16[1,2,1,6144,128]{4,3,2,1,0:T(8,128)(2,1)S(1)} copy-done((bf16[1,2,1,6144,128]{4,3,2,1,0:T(8,128)(2,1)S(1)}, bf16[1,2,1,6144,128]{4,3,2,1,0:T(8,128)(2,1)}, u32[]{:S(2)}) %copy-start) | copy-done | bytes 3145752
  2.5 0.0 copy-start.1
  2.5 0.4 shard_map.76
  2.9 2.1 %collective-permute-start = (f32[4,2,6,64,128]{4,3,2,1,0:T(8,128)S(1)}, f32[4,2,6,64,128]{4,3,2,1,0:T(8,128)S(1)}, u32[]{:S(2)}, u32[]{:S(2)}) collective-permute-start(f32[4,2,6,64,128]{4,3,2,1,0:T(8,128)S(1)} %shard_map.76), channel_id=1, source_target_pairs={{0,8},{8,0},{16,24},{24,16},{32,40},{40,32},{48,56},{56,48},{64,72... | collective-permute-start | bytes 4718600 | tf_op jit(solution)/shard_map/ppermute | solution.py:134
  5.0 3.4 %collective-permute-done.got_ref = f32[4,2,6,64,128]{4,3,2,1,0:T(8,128)S(1)} collective-permute-done((f32[4,2,6,64,128]{4,3,2,1,0:T(8,128)S(1)}, f32[4,2,6,64,128]{4,3,2,1,0:T(8,128)S(1)}, u32[]{:S(2)}, u32[]{:S(2)}) %collective-permute-start) | collective-permute-done | bytes 1572896 | tf_op jit(solution)/shard_map/ppermute | solution.py:134
  8.3 0.0 copy-done.1
  8.3 0.4 shard_map.77
  8.8 31.4 %all_to_all.15 = f32[8,384,128]{2,1,0:T(8,128)S(1)} all-to-all(f32[8,384,128]{2,1,0:T(8,128)S(1)} %bitcast.10), channel_id=1, replica_groups={{0,16,192,208,384,400,576,592},{8,24,200,216,392,408,584,600},{32,48,22..., dimensions={0} | all-to-all | bytes 3145728 | tf_op jit(solution)/shard_map/all_to_all | solution.py:136
  40.2 0.0 copy-start.2
  40.2 0.0 copy-start.3
  40.2 0.0 copy-start.4
  40.2 0.0 copy-start.5
  40.2 0.1 reduce_sum.9
  40.3 20.3 %all_to_all.16.parts_ref = f32[6,64,128]{2,1,0:T(8,128)S(1)} all-to-all(f32[6,64,128]{2,1,0:T(8,128)S(1)} %bitcast.15), channel_id=1, replica_groups={{0,32,64,96,128,160},{8,40,72,104,136,168},{16,48,80,112,144,176},{24,5..., dimensions={0} | all-to-all | bytes 393216 | tf_op jit(solution)/shard_map/all_to_all | solution.py:140
  60.6 0.0 copy-done.2
  60.6 0.0 copy-done.3
  60.6 0.0 copy-done.4
  60.6 0.0 copy-done.5
  60.6 0.7 shard_map.78
  61.3 19.1 %all_to_all.17.got_ref = f32[8,104,128]{2,1,0:T(8,128)S(1)} all-to-all(f32[8,104,128]{2,1,0:T(8,128)S(1)} %shard_map.78), channel_id=1, replica_groups=mesh['dp'=96,'section'=8] {'section'}, dimensions={0} | all-to-all | bytes 851968 | tf_op jit(solution)/shard_map/all_to_all | solution.py:148
  80.4 0.9 %shard_map.79 = (f32[1,256,128]{2,1,0:T(8,128)}, f32[1,256,128]{2,1,0:T(8,128)}, f32[1,256,128]{2,1,0:T(8,128)}) custom-call(f32[8,104,128]{2,1,0:T(8,128)S(1)} %all_to_all.17.got_ref), custom_call_target="tpu_custom_call" | custom-call | tf_op jit(solution)/shard_map/pallas_call | solution.py:150
Async XLA Ops:
  0.6 1.9 %copy-start = (bf16[1,2,1,6144,128]{4,3,2,1,0:T(8,128)(2,1)S(1)}, bf16[1,2,1,6144,128]{4,3,2,1,0:T(8,128)(2,1)}, u32[]{:S(2)}) copy-start(bf16[1,2,1,6144,128]{4,3,2,1,0:T(8,128)(2,1)} %param.5) | copy-start | bytes 9437188
  2.5 5.8 %copy-start.1 = (bf16[1,2,1,6144,128]{4,3,2,1,0:T(8,128)(2,1)S(1)}, bf16[1,2,1,6144,128]{4,3,2,1,0:T(8,128)(2,1)}, u32[]{:S(2)}) copy-start(bf16[1,2,1,6144,128]{4,3,2,1,0:T(8,128)(2,1)} %param.5) | copy-start | bytes 9437188
  2.9 5.4 %collective-permute-start = (f32[4,2,6,64,128]{4,3,2,1,0:T(8,128)S(1)}, f32[4,2,6,64,128]{4,3,2,1,0:T(8,128)S(1)}, u32[]{:S(2)}, u32[]{:S(2)}) collective-permute-start(f32[4,2,6,64,128]{4,3,2,1,0:T(8,128)S(1)} %shard_map.76), channel_id=1, source_target_pairs={{0,8},{8,0},{16,24},{24,16},{32,40},{40,32},{48,56},{56,48},{64,72... | collective-permute-start | bytes 4718600 | tf_op jit(solution)/shard_map/ppermute | solution.py:134
  40.2 20.4 %copy-start.2 = (f32[1,64,128]{2,1,0:T(8,128)S(1)}, f32[1,64,128]{2,1,0:T(8,128)}, u32[]{:S(2)}) copy-start(f32[1,64,128]{2,1,0:T(8,128)} %param.6) | copy-start | bytes 98308
  40.2 20.4 %copy-start.3 = (f32[1,64,128]{2,1,0:T(8,128)S(1)}, f32[1,64,128]{2,1,0:T(8,128)}, u32[]{:S(2)}) copy-start(f32[1,64,128]{2,1,0:T(8,128)} %param.7) | copy-start | bytes 98308
  40.2 20.4 %copy-start.4 = (f32[1,64,128]{2,1,0:T(8,128)S(1)}, f32[1,64,128]{2,1,0:T(8,128)}, u32[]{:S(2)}) copy-start(f32[1,64,128]{2,1,0:T(8,128)} %param.8) | copy-start | bytes 98308
  40.2 20.4 %copy-start.5 = (s32[1,1,8]{2,1,0:T(1,128)S(1)}, s32[1,1,8]{2,1,0:T(1,128)}, u32[]{:S(2)}) copy-start(s32[1,1,8]{2,1,0:T(1,128)} %param.9) | copy-start | bytes 100

commit v3 on v1

--- a/solution.py
+++ b/solution.py
@@ -18,8 +18,10 @@
 ROWS = 64
 PIECES, PIECE = 8, 8
 WRITERS, CAP = 8, 4
-STATE = 3 * CAP * PIECE
-BLOCK = STATE + PIECE
+HELD = CAP * PIECE
+BLOCK = 3 * HELD
+EMPTY = -1.0
+LIMIT = 8 * 1024 * 1024
 
 
 def device_of(x, z, core):
@@ -28,7 +30,7 @@
 
 def near_groups():
     return [
-        [device_of(x, PAIR * a + b, c) for x in range(X) for b in range(PAIR)]
+        [device_of(x, PAIR * a + b, c) for b in range(PAIR) for x in range(X)]
         for a in range(FAR)
         for c in range(CORE)
     ]
@@ -43,39 +45,41 @@
     ]
 
 
+def summed(grads_ref, x, a):
+    first = grads_ref[0, x, a, 0, 0].astype(jnp.float32)
+    return first + grads_ref[1, x, a, 0, 0].astype(jnp.float32)
+
+
 def send_kernel(core_ref, grads_ref, out_ref):
-    for a in range(FAR):
-        for b in range(PAIR):
-            first = grads_ref[0, 0, a, b, 0].astype(jnp.float32)
-            out_ref[0, b, a] = first + grads_ref[1, 0, a, b, 0].astype(jnp.float32)
+    for x in range(X):
+        for a in range(FAR):
+            out_ref[0, x, a] = summed(grads_ref, x, a)
 
 
 def join_kernel(core_ref, grads_ref, got_ref, out_ref):
-    for a in range(FAR):
-        for b in range(PAIR):
-            first = grads_ref[0, 0, a, b, 0].astype(jnp.float32)
-            own = first + grads_ref[1, 0, a, b, 0].astype(jnp.float32)
-            out_ref[0, b, a] = own + got_ref[0, b, a]
+    for x in range(X):
+        for a in range(FAR):
+            out_ref[0, x, a] = summed(grads_ref, x, a) + got_ref[0, x, a]
 
 
 def half_call(kernel, core, grads, *got):
-    block = (1, PAIR, FAR, ROWS, LANE)
-    stream = pl.BlockSpec(block, lambda i, core_ref: (i, 0, 0, 0, 0))
+    stream = pl.BlockSpec((1, X, FAR, ROWS, LANE), lambda b, core_ref: (b, 0, 0, 0, 0))
     return pl.pallas_call(
         kernel,
-        out_shape=jax.ShapeDtypeStruct((X, PAIR, FAR, ROWS, LANE), jnp.float32),
+        out_shape=jax.ShapeDtypeStruct((PAIR, X, FAR, ROWS, LANE), jnp.float32),
         grid_spec=pltpu.PrefetchScalarGridSpec(
             num_scalar_prefetch=1,
-            grid=(X,),
+            grid=(PAIR,),
             in_specs=[
                 pl.BlockSpec(
-                    (2, 1, FAR, PAIR, 1, ROWS, LANE),
-                    lambda i, core_ref: (0, i, 0, 0, core_ref[0], 0, 0),
+                    (2, X, FAR, 1, 1, ROWS, LANE),
+                    lambda b, core_ref: (0, 0, 0, b, core_ref[0], 0, 0),
                 )
             ]
             + [stream] * len(got),
             out_specs=stream,
         ),
+        compiler_params=pltpu.CompilerParams(vmem_limit_bytes=LIMIT),
         cost_estimate=pl.CostEstimate(
             flops=2 * X * Z * ROWS * LANE,
             bytes_accessed=(8 + 4 * len(got)) * X * Z * ROWS * LANE,
@@ -95,10 +99,8 @@
         momentum / (jnp.sqrt(variance) + epsilon) + decay_rate * weights
     )
     owners = [owner_ref[p] for p in range(PIECES)]
-    out_ref[...] = jnp.zeros_like(out_ref)
-    for w in range(WRITERS):
-        count = sum((owner == w).astype(jnp.int32) for owner in owners)
-        out_ref[w, STATE:BLOCK] = jnp.full((PIECE, LANE), count.astype(jnp.float32))
+    out_ref[:, : 2 * HELD] = jnp.zeros((WRITERS, 2 * HELD, LANE), jnp.float32)
+    out_ref[:, 2 * HELD :] = jnp.full((WRITERS, HELD, LANE), EMPTY)
     for p in range(PIECES):
         slot = jnp.int32(0)
         for q in range(p):
@@ -115,20 +117,25 @@
         out_ref[...] = jnp.zeros_like(out_ref)
     start = jnp.int32(0)
     for s in range(WRITERS):
-        at = pl.multiple_of(start * PIECE, PIECE)
-        for k, out_ref in enumerate(outs):
-            rows = slice(k * CAP * PIECE, (k + 1) * CAP * PIECE)
-            out_ref[0, pl.ds(at, CAP * PIECE)] = got_ref[s, rows]
+        at = pl.ds(pl.multiple_of(start * PIECE, PIECE), HELD)
+        variance = got_ref[s, 2 * HELD :]
+        param_ref[0, at] = got_ref[s, :HELD]
+        first_ref[0, at] = got_ref[s, HELD : 2 * HELD]
+        second_ref[0, at] = jnp.maximum(variance, 0.0)
         if s < WRITERS - 1:
-            start = start + jnp.max(got_ref[s, STATE:BLOCK]).astype(jnp.int32)
+            taken = sum(
+                (variance[c * PIECE : (c + 1) * PIECE] >= 0.0).astype(jnp.int32)
+                for c in range(CAP)
+            )
+            start = start + jnp.max(taken)
 
 
 def body(grads, params, first_moment, second_moment, owners):
     vmem = pl.BlockSpec(memory_space=pltpu.VMEM)
     smem = pl.BlockSpec(memory_space=pltpu.SMEM)
-    core = lax.rem(lax.axis_index("dp"), CORE).astype(jnp.int32).reshape(1)
+    core = (lax.axis_index("dp").astype(jnp.int32) & 1).reshape(1)
     grads = grads.reshape(2, X, FAR, PAIR, CORE, ROWS, LANE)
-    sent = half_call(send_kernel, 1 - core, grads)
+    sent = half_call(send_kernel, core ^ 1, grads)
     swap = [(i, i ^ 1) for i in range(X * Z * CORE)]
     got = lax.ppermute(sent, "dp", swap)
     chip = half_call(join_kernel, core, grads, got)
@@ -142,6 +149,7 @@
         out_shape=jax.ShapeDtypeStruct((WRITERS, BLOCK, LANE), jnp.float32),
         in_specs=[smem] + [vmem] * 4,
         out_specs=vmem,
+        compiler_params=pltpu.CompilerParams(vmem_limit_bytes=LIMIT),
     )(owners.reshape(PIECES), far, params[0], first_moment[0], second_moment[0])
     handed = lax.all_to_all(packed, "section", 0, 0)
     out = jax.ShapeDtypeStruct((1, WRITERS * CAP * PIECE, LANE), jnp.float32)
@@ -150,6 +158,7 @@
         out_shape=(out,) * 3,
         in_specs=[vmem],
         out_specs=(vmem,) * 3,
+        compiler_params=pltpu.CompilerParams(vmem_limit_bytes=LIMIT),
     )(handed)
 
 

time: 91 us -> 81.4 us (0.89)
  Pallas kernels: 11.2 us -> 2.26 us
    pallas_call x2, Pallas kernels: 7.53 us -> 0.69 us  [half_call(): pl.pallas_call(kernel, out_shape=jax.ShapeDtypeStruct((PAIR, X, FAR, ROWS...]
    pallas_call x1, Pallas kernels: 1.83 us -> 0.6 us  [body(): pl.pallas_call(pack_kernel, out_shape=jax.ShapeDtypeStruct((WRITERS, BLOC...]
    all_to_all x1, blocking collectives: 32.5 us -> 31.3 us  [body(): lax.all_to_all(chip.reshape(X * PAIR, FAR * ROWS, LANE), 'dp', 0, 0, axis...]
    all_to_all x1, blocking collectives: 19.5 us -> 20.6 us  [body(): far = lax.all_to_all(near, 'dp', 0, 0, axis_index_groups=far_groups())]
    unnamed x2 -> x12, local copies, waits for them, and re-layouts: 1.15 us -> 1.9 us
where the time goes in v3:
time: 81.4 us; the launch traced here: 81.1 us
  blocking collectives  70.7 us (87%)
  waiting for transfers between devices  3.38 us (4%)
  Pallas kernels  2.26 us (3%)
  starting transfers between devices  2.05 us (3%)
  local copies, waits for them, and re-layouts  1.9 us (2%)
    all_to_all x1, blocking collectives, body(): lax.all_to_all(chip.reshape(X * PAIR, FAR * ROWS, LANE), 'dp', 0, 0, axis...  31.3 us
    all_to_all x1, blocking collectives, body(): far = lax.all_to_all(near, 'dp', 0, 0, axis_index_groups=far_groups())  20.6 us
    all_to_all x1, blocking collectives, body(): handed = lax.all_to_all(packed, 'section', 0, 0)  18.8 us
    ppermute x1, waiting for transfers between devices, body(): got = lax.ppermute(sent, 'dp', swap)  3.38 us
    ppermute x1, starting transfers between devices, body(): got = lax.ppermute(sent, 'dp', swap)  2.05 us
    unnamed x12, local copies, waits for them, and re-layouts  1.9 us
  transfers between devices with their start and end apart: 1, of which 1 were waited for; matrix products, arithmetic and copies ran while one was open for 0% of the time, Pallas kernels for 0%

profile of v3, /device:TPU:6, one launch (start us, length us, event | category | flops | bytes accessed | tf_op | source)
XLA Modules:
  0.0 81.1 jit_solution(7035028344264659933)
XLA Ops:
  0.6 0.0 copy-start
  0.7 1.9 %copy-done = bf16[1,2,1,6144,128]{4,3,2,1,0:T(8,128)(2,1)S(1)} copy-done((bf16[1,2,1,6144,128]{4,3,2,1,0:T(8,128)(2,1)S(1)}, bf16[1,2,1,6144,128]{4,3,2,1,0:T(8,128)(2,1)}, u32[]{:S(2)}) %copy-start) | copy-done | bytes 3145752
  2.5 0.0 copy-start.1
  2.5 0.3 shard_map.76
  2.9 2.1 %collective-permute-start = (f32[2,4,6,64,128]{4,3,2,1,0:T(8,128)S(1)}, f32[2,4,6,64,128]{4,3,2,1,0:T(8,128)S(1)}, u32[]{:S(2)}, u32[]{:S(2)}) collective-permute-start(f32[2,4,6,64,128]{4,3,2,1,0:T(8,128)S(1)} %shard_map.76), channel_id=1, source_target_pairs={{0,8},{8,0},{16,24},{24,16},{32,40},{40,32},{48,56},{56,48},{64,72... | collective-permute-start | bytes 4718600 | tf_op jit(solution)/shard_map/ppermute | solution.py:140
  4.9 3.4 %collective-permute-done.got_ref = f32[2,4,6,64,128]{4,3,2,1,0:T(8,128)S(1)} collective-permute-done((f32[2,4,6,64,128]{4,3,2,1,0:T(8,128)S(1)}, f32[2,4,6,64,128]{4,3,2,1,0:T(8,128)S(1)}, u32[]{:S(2)}, u32[]{:S(2)}) %collective-permute-start) | collective-permute-done | bytes 1572896 | tf_op jit(solution)/shard_map/ppermute | solution.py:140
  8.3 0.0 copy-done.1
  8.3 0.4 shard_map.77
  8.7 31.3 %all_to_all.15 = f32[8,384,128]{2,1,0:T(8,128)S(1)} all-to-all(f32[8,384,128]{2,1,0:T(8,128)S(1)} %bitcast.10), channel_id=1, replica_groups={{0,192,384,576,16,208,400,592},{8,200,392,584,24,216,408,600},{32,224,4..., dimensions={0} | all-to-all | bytes 3145728 | tf_op jit(solution)/shard_map/all_to_all | solution.py:142
  40.0 0.0 copy-start.2
  40.0 0.0 copy-start.3
  40.0 0.0 copy-start.4
  40.0 0.0 copy-start.5
  40.0 0.1 reduce_sum.9
  40.1 20.6 %all_to_all.16.parts_ref = f32[6,64,128]{2,1,0:T(8,128)S(1)} all-to-all(f32[6,64,128]{2,1,0:T(8,128)S(1)} %bitcast.15), channel_id=1, replica_groups={{0,32,64,96,128,160},{8,40,72,104,136,168},{16,48,80,112,144,176},{24,5..., dimensions={0} | all-to-all | bytes 393216 | tf_op jit(solution)/shard_map/all_to_all | solution.py:146
  60.7 0.0 copy-done.2
  60.7 0.0 copy-done.3
  60.7 0.0 copy-done.4
  60.7 0.0 copy-done.5
  60.7 0.6 shard_map.78
  61.3 18.8 %all_to_all.17.got_ref = f32[8,96,128]{2,1,0:T(8,128)S(1)} all-to-all(f32[8,96,128]{2,1,0:T(8,128)S(1)} %shard_map.78), channel_id=1, replica_groups=mesh['dp'=96,'section'=8] {'section'}, dimensions={0} | all-to-all | bytes 786432 | tf_op jit(solution)/shard_map/all_to_all | solution.py:154
  80.1 1.0 %shard_map.79 = (f32[1,256,128]{2,1,0:T(8,128)}, f32[1,256,128]{2,1,0:T(8,128)}, f32[1,256,128]{2,1,0:T(8,128)}) custom-call(f32[8,96,128]{2,1,0:T(8,128)S(1)} %all_to_all.17.got_ref), custom_call_target="tpu_custom_call" | custom-call | tf_op jit(solution)/shard_map/pallas_call | solution.py:156
Async XLA Ops:
  0.6 1.9 %copy-start = (bf16[1,2,1,6144,128]{4,3,2,1,0:T(8,128)(2,1)S(1)}, bf16[1,2,1,6144,128]{4,3,2,1,0:T(8,128)(2,1)}, u32[]{:S(2)}) copy-start(bf16[1,2,1,6144,128]{4,3,2,1,0:T(8,128)(2,1)} %param.5) | copy-start | bytes 9437188
  2.5 5.8 %copy-start.1 = (bf16[1,2,1,6144,128]{4,3,2,1,0:T(8,128)(2,1)S(1)}, bf16[1,2,1,6144,128]{4,3,2,1,0:T(8,128)(2,1)}, u32[]{:S(2)}) copy-start(bf16[1,2,1,6144,128]{4,3,2,1,0:T(8,128)(2,1)} %param.5) | copy-start | bytes 9437188
  2.9 5.4 %collective-permute-start = (f32[2,4,6,64,128]{4,3,2,1,0:T(8,128)S(1)}, f32[2,4,6,64,128]{4,3,2,1,0:T(8,128)S(1)}, u32[]{:S(2)}, u32[]{:S(2)}) collective-permute-start(f32[2,4,6,64,128]{4,3,2,1,0:T(8,128)S(1)} %shard_map.76), channel_id=1, source_target_pairs={{0,8},{8,0},{16,24},{24,16},{32,40},{40,32},{48,56},{56,48},{64,72... | collective-permute-start | bytes 4718600 | tf_op jit(solution)/shard_map/ppermute | solution.py:140
  40.0 20.7 %copy-start.2 = (f32[1,64,128]{2,1,0:T(8,128)S(1)}, f32[1,64,128]{2,1,0:T(8,128)}, u32[]{:S(2)}) copy-start(f32[1,64,128]{2,1,0:T(8,128)} %param.6) | copy-start | bytes 98308
  40.0 20.7 %copy-start.3 = (f32[1,64,128]{2,1,0:T(8,128)S(1)}, f32[1,64,128]{2,1,0:T(8,128)}, u32[]{:S(2)}) copy-start(f32[1,64,128]{2,1,0:T(8,128)} %param.7) | copy-start | bytes 98308
  40.0 20.7 %copy-start.4 = (f32[1,64,128]{2,1,0:T(8,128)S(1)}, f32[1,64,128]{2,1,0:T(8,128)}, u32[]{:S(2)}) copy-start(f32[1,64,128]{2,1,0:T(8,128)} %param.8) | copy-start | bytes 98308
  40.0 20.7 %copy-start.5 = (s32[1,1,8]{2,1,0:T(1,128)S(1)}, s32[1,1,8]{2,1,0:T(1,128)}, u32[]{:S(2)}) copy-start(s32[1,1,8]{2,1,0:T(1,128)} %param.9) | copy-start | bytes 100

commit v4 on v3

--- a/solution.py
+++ b/solution.py
@@ -28,9 +28,13 @@
     return (x * Z + z) * CORE + core
 
 
+def z_of(a, side):
+    return PAIR * a + (side ^ (a % 2))
+
+
 def near_groups():
     return [
-        [device_of(x, PAIR * a + b, c) for b in range(PAIR) for x in range(X)]
+        [device_of(x, z_of(a, side), c) for side in range(PAIR) for x in range(X)]
         for a in range(FAR)
         for c in range(CORE)
     ]
@@ -38,45 +42,45 @@
 
 def far_groups():
     return [
-        [device_of(x, PAIR * a + b, c) for a in range(FAR)]
+        [device_of(x, z_of(a, side), c) for a in range(FAR)]
         for x in range(X)
-        for b in range(PAIR)
+        for side in range(PAIR)
         for c in range(CORE)
     ]
 
 
-def summed(grads_ref, x, a):
-    first = grads_ref[0, x, a, 0, 0].astype(jnp.float32)
-    return first + grads_ref[1, x, a, 0, 0].astype(jnp.float32)
+def summed(grads_ref, x, k):
+    first = grads_ref[0, x, k, 0, 0, 0].astype(jnp.float32)
+    return first + grads_ref[1, x, k, 0, 0, 0].astype(jnp.float32)
 
 
-def send_kernel(core_ref, grads_ref, out_ref):
+def send_kernel(core_ref, even_ref, odd_ref, out_ref):
     for x in range(X):
-        for a in range(FAR):
-            out_ref[0, x, a] = summed(grads_ref, x, a)
+        for k in range(FAR // 2):
+            for parity, grads_ref in enumerate((even_ref, odd_ref)):
+                out_ref[0, x, 2 * k + parity] = summed(grads_ref, x, k)
 
 
-def join_kernel(core_ref, grads_ref, got_ref, out_ref):
+def join_kernel(core_ref, even_ref, odd_ref, got_ref, out_ref):
     for x in range(X):
-        for a in range(FAR):
-            out_ref[0, x, a] = summed(grads_ref, x, a) + got_ref[0, x, a]
+        for k in range(FAR // 2):
+            for parity, grads_ref in enumerate((even_ref, odd_ref)):
+                a = 2 * k + parity
+                out_ref[0, x, a] = summed(grads_ref, x, k) + got_ref[0, x, a]
 
 
 def half_call(kernel, core, grads, *got):
-    stream = pl.BlockSpec((1, X, FAR, ROWS, LANE), lambda b, core_ref: (b, 0, 0, 0, 0))
+    stream = pl.BlockSpec((1, X, FAR, ROWS, LANE), lambda side, core_ref: (side, 0, 0, 0, 0))
+    block = (2, X, FAR // 2, 1, 1, 1, ROWS, LANE)
+    even = pl.BlockSpec(block, lambda side, core_ref: (0, 0, 0, 0, side, core_ref[0], 0, 0))
+    odd = pl.BlockSpec(block, lambda side, core_ref: (0, 0, 0, 1, 1 - side, core_ref[0], 0, 0))
     return pl.pallas_call(
         kernel,
         out_shape=jax.ShapeDtypeStruct((PAIR, X, FAR, ROWS, LANE), jnp.float32),
         grid_spec=pltpu.PrefetchScalarGridSpec(
             num_scalar_prefetch=1,
             grid=(PAIR,),
-            in_specs=[
-                pl.BlockSpec(
-                    (2, X, FAR, 1, 1, ROWS, LANE),
-                    lambda b, core_ref: (0, 0, 0, b, core_ref[0], 0, 0),
-                )
-            ]
-            + [stream] * len(got),
+            in_specs=[even, odd] + [stream] * len(got),
             out_specs=stream,
         ),
         compiler_params=pltpu.CompilerParams(vmem_limit_bytes=LIMIT),
@@ -85,7 +89,7 @@
             bytes_accessed=(8 + 4 * len(got)) * X * Z * ROWS * LANE,
             transcendentals=0,
         ),
-    )(core, grads, *got)
+    )(core, grads, grads, *got)
 
 
 def pack_kernel(owner_ref, parts_ref, params_ref, first_ref, second_ref, out_ref):
@@ -134,7 +138,7 @@
     vmem = pl.BlockSpec(memory_space=pltpu.VMEM)
     smem = pl.BlockSpec(memory_space=pltpu.SMEM)
     core = (lax.axis_index("dp").astype(jnp.int32) & 1).reshape(1)
-    grads = grads.reshape(2, X, FAR, PAIR, CORE, ROWS, LANE)
+    grads = grads.reshape(2, X, FAR // 2, 2, PAIR, CORE, ROWS, LANE)
     sent = half_call(send_kernel, core ^ 1, grads)
     swap = [(i, i ^ 1) for i in range(X * Z * CORE)]
     got = lax.ppermute(sent, "dp", swap)

time: 81.4 us -> 81 us (level)
    all_to_all x1, blocking collectives: 20.6 us -> 19.7 us  [body(): far = lax.all_to_all(near, 'dp', 0, 0, axis_index_groups=far_groups())]
where the time goes in v4:
time: 81 us; the launch traced here: 80.3 us
  blocking collectives  69.9 us (86%)
  waiting for transfers between devices  3.38 us (4%)
  Pallas kernels  2.3 us (3%)
  starting transfers between devices  2.05 us (3%)
  local copies, waits for them, and re-layouts  1.9 us (2%)
    all_to_all x1, blocking collectives, body(): lax.all_to_all(chip.reshape(X * PAIR, FAR * ROWS, LANE), 'dp', 0, 0, axis...  31.3 us
    all_to_all x1, blocking collectives, body(): far = lax.all_to_all(near, 'dp', 0, 0, axis_index_groups=far_groups())  19.7 us
    all_to_all x1, blocking collectives, body(): handed = lax.all_to_all(packed, 'section', 0, 0)  18.8 us
    ppermute x1, waiting for transfers between devices, body(): got = lax.ppermute(sent, 'dp', swap)  3.38 us
    ppermute x1, starting transfers between devices, body(): got = lax.ppermute(sent, 'dp', swap)  2.05 us
    unnamed x12, local copies, waits for them, and re-layouts  1.9 us
  transfers between devices with their start and end apart: 1, of which 1 were waited for; matrix products, arithmetic and copies ran while one was open for 0% of the time, Pallas kernels for 0%

profile of v4, /device:TPU:6, one launch (start us, length us, event | category | flops | bytes accessed | tf_op | source)
XLA Modules:
  0.0 80.3 jit_solution(4162944958406613955)
XLA Ops:
  0.6 0.0 copy-start
  0.7 1.9 %copy-done = bf16[1,2,1,6144,128]{4,3,2,1,0:T(8,128)(2,1)S(1)} copy-done((bf16[1,2,1,6144,128]{4,3,2,1,0:T(8,128)(2,1)S(1)}, bf16[1,2,1,6144,128]{4,3,2,1,0:T(8,128)(2,1)}, u32[]{:S(2)}) %copy-start) | copy-done | bytes 3145752
  2.5 0.0 copy-start.1
  2.5 0.3 shard_map.76
  2.9 2.1 %collective-permute-start = (f32[2,4,6,64,128]{4,3,2,1,0:T(8,128)S(1)}, f32[2,4,6,64,128]{4,3,2,1,0:T(8,128)S(1)}, u32[]{:S(2)}, u32[]{:S(2)}) collective-permute-start(f32[2,4,6,64,128]{4,3,2,1,0:T(8,128)S(1)} %shard_map.76), channel_id=1, source_target_pairs={{0,8},{8,0},{16,24},{24,16},{32,40},{40,32},{48,56},{56,48},{64,72... | collective-permute-start | bytes 4718600 | tf_op jit(solution)/shard_map/ppermute | solution.py:144
  4.9 3.4 %collective-permute-done.got_ref = f32[2,4,6,64,128]{4,3,2,1,0:T(8,128)S(1)} collective-permute-done((f32[2,4,6,64,128]{4,3,2,1,0:T(8,128)S(1)}, f32[2,4,6,64,128]{4,3,2,1,0:T(8,128)S(1)}, u32[]{:S(2)}, u32[]{:S(2)}) %collective-permute-start) | collective-permute-done | bytes 1572896 | tf_op jit(solution)/shard_map/ppermute | solution.py:144
  8.3 0.0 copy-done.1
  8.3 0.4 shard_map.77
  8.7 31.3 %all_to_all.15 = f32[8,384,128]{2,1,0:T(8,128)S(1)} all-to-all(f32[8,384,128]{2,1,0:T(8,128)S(1)} %bitcast.12), channel_id=1, replica_groups={{0,192,384,576,16,208,400,592},{8,200,392,584,24,216,408,600},{48,240,4..., dimensions={0} | all-to-all | bytes 3145728 | tf_op jit(solution)/shard_map/all_to_all | solution.py:146
  40.1 0.0 copy-start.2
  40.1 0.0 copy-start.3
  40.1 0.0 copy-start.4
  40.1 0.0 copy-start.5
  40.1 0.1 reduce_sum.9
  40.2 19.7 %all_to_all.16.parts_ref = f32[6,64,128]{2,1,0:T(8,128)S(1)} all-to-all(f32[6,64,128]{2,1,0:T(8,128)S(1)} %bitcast.17), channel_id=1, replica_groups={{0,48,64,112,128,176},{8,56,72,120,136,184},{16,32,80,96,144,160},{24,4..., dimensions={0} | all-to-all | bytes 393216 | tf_op jit(solution)/shard_map/all_to_all | solution.py:150
  59.9 0.0 copy-done.2
  59.9 0.0 copy-done.3
  59.9 0.0 copy-done.4
  59.9 0.0 copy-done.5
  59.9 0.6 shard_map.78
  60.5 18.8 %all_to_all.17.got_ref = f32[8,96,128]{2,1,0:T(8,128)S(1)} all-to-all(f32[8,96,128]{2,1,0:T(8,128)S(1)} %shard_map.78), channel_id=1, replica_groups=mesh['dp'=96,'section'=8] {'section'}, dimensions={0} | all-to-all | bytes 786432 | tf_op jit(solution)/shard_map/all_to_all | solution.py:158
  79.3 1.0 %shard_map.79 = (f32[1,256,128]{2,1,0:T(8,128)}, f32[1,256,128]{2,1,0:T(8,128)}, f32[1,256,128]{2,1,0:T(8,128)}) custom-call(f32[8,96,128]{2,1,0:T(8,128)S(1)} %all_to_all.17.got_ref), custom_call_target="tpu_custom_call" | custom-call | tf_op jit(solution)/shard_map/pallas_call | solution.py:160
Async XLA Ops:
  0.6 1.9 %copy-start = (bf16[1,2,1,6144,128]{4,3,2,1,0:T(8,128)(2,1)S(1)}, bf16[1,2,1,6144,128]{4,3,2,1,0:T(8,128)(2,1)}, u32[]{:S(2)}) copy-start(bf16[1,2,1,6144,128]{4,3,2,1,0:T(8,128)(2,1)} %param.5) | copy-start | bytes 9437188
  2.5 5.8 %copy-start.1 = (bf16[1,2,1,6144,128]{4,3,2,1,0:T(8,128)(2,1)S(1)}, bf16[1,2,1,6144,128]{4,3,2,1,0:T(8,128)(2,1)}, u32[]{:S(2)}) copy-start(bf16[1,2,1,6144,128]{4,3,2,1,0:T(8,128)(2,1)} %param.5) | copy-start | bytes 9437188
  2.9 5.4 %collective-permute-start = (f32[2,4,6,64,128]{4,3,2,1,0:T(8,128)S(1)}, f32[2,4,6,64,128]{4,3,2,1,0:T(8,128)S(1)}, u32[]{:S(2)}, u32[]{:S(2)}) collective-permute-start(f32[2,4,6,64,128]{4,3,2,1,0:T(8,128)S(1)} %shard_map.76), channel_id=1, source_target_pairs={{0,8},{8,0},{16,24},{24,16},{32,40},{40,32},{48,56},{56,48},{64,72... | collective-permute-start | bytes 4718600 | tf_op jit(solution)/shard_map/ppermute | solution.py:144
  40.1 19.8 %copy-start.2 = (f32[1,64,128]{2,1,0:T(8,128)S(1)}, f32[1,64,128]{2,1,0:T(8,128)}, u32[]{:S(2)}) copy-start(f32[1,64,128]{2,1,0:T(8,128)} %param.6) | copy-start | bytes 98308
  40.1 19.8 %copy-start.3 = (f32[1,64,128]{2,1,0:T(8,128)S(1)}, f32[1,64,128]{2,1,0:T(8,128)}, u32[]{:S(2)}) copy-start(f32[1,64,128]{2,1,0:T(8,128)} %param.7) | copy-start | bytes 98308
  40.1 19.8 %copy-start.4 = (f32[1,64,128]{2,1,0:T(8,128)S(1)}, f32[1,64,128]{2,1,0:T(8,128)}, u32[]{:S(2)}) copy-start(f32[1,64,128]{2,1,0:T(8,128)} %param.8) | copy-start | bytes 98308
  40.1 19.9 %copy-start.5 = (s32[1,1,8]{2,1,0:T(1,128)S(1)}, s32[1,1,8]{2,1,0:T(1,128)}, u32[]{:S(2)}) copy-start(s32[1,1,8]{2,1,0:T(1,128)} %param.9) | copy-start | bytes 100

commit v5 on v4

--- a/solution.py
+++ b/solution.py
@@ -49,47 +49,40 @@
     ]
 
 
-def summed(grads_ref, x, k):
-    first = grads_ref[0, x, k, 0, 0, 0].astype(jnp.float32)
-    return first + grads_ref[1, x, k, 0, 0, 0].astype(jnp.float32)
+def summed(grads_ref, core, side, x, a):
+    at = (x, a // 2, a % 2, side ^ (a % 2), core)
+    return grads_ref[(0, *at)].astype(jnp.float32) + grads_ref[(1, *at)].astype(jnp.float32)
 
 
-def send_kernel(core_ref, even_ref, odd_ref, out_ref):
-    for x in range(X):
-        for k in range(FAR // 2):
-            for parity, grads_ref in enumerate((even_ref, odd_ref)):
-                out_ref[0, x, 2 * k + parity] = summed(grads_ref, x, k)
+def send_kernel(core_ref, grads_ref, out_ref):
+    for side in range(PAIR):
+        for x in range(X):
+            for a in range(FAR):
+                out_ref[side, x, a] = summed(grads_ref, core_ref[0], side, x, a)
 
 
-def join_kernel(core_ref, even_ref, odd_ref, got_ref, out_ref):
-    for x in range(X):
-        for k in range(FAR // 2):
-            for parity, grads_ref in enumerate((even_ref, odd_ref)):
-                a = 2 * k + parity
-                out_ref[0, x, a] = summed(grads_ref, x, k) + got_ref[0, x, a]
+def join_kernel(core_ref, grads_ref, got_ref, out_ref):
+    for side in range(PAIR):
+        for x in range(X):
+            for a in range(FAR):
+                own = summed(grads_ref, core_ref[0], side, x, a)
+                out_ref[side, x, a] = own + got_ref[side, x, a]
 
 
 def half_call(kernel, core, grads, *got):
-    stream = pl.BlockSpec((1, X, FAR, ROWS, LANE), lambda side, core_ref: (side, 0, 0, 0, 0))
-    block = (2, X, FAR // 2, 1, 1, 1, ROWS, LANE)
-    even = pl.BlockSpec(block, lambda side, core_ref: (0, 0, 0, 0, side, core_ref[0], 0, 0))
-    odd = pl.BlockSpec(block, lambda side, core_ref: (0, 0, 0, 1, 1 - side, core_ref[0], 0, 0))
+    vmem = pl.BlockSpec(memory_space=pltpu.VMEM)
     return pl.pallas_call(
         kernel,
         out_shape=jax.ShapeDtypeStruct((PAIR, X, FAR, ROWS, LANE), jnp.float32),
-        grid_spec=pltpu.PrefetchScalarGridSpec(
-            num_scalar_prefetch=1,
-            grid=(PAIR,),
-            in_specs=[even, odd] + [stream] * len(got),
-            out_specs=stream,
-        ),
-        compiler_params=pltpu.CompilerParams(vmem_limit_bytes=LIMIT),
+        in_specs=[pl.BlockSpec(memory_space=pltpu.SMEM), vmem] + [vmem] * len(got),
+        out_specs=vmem,
+        compiler_params=pltpu.CompilerParams(vmem_limit_bytes=2 * LIMIT),
         cost_estimate=pl.CostEstimate(
             flops=2 * X * Z * ROWS * LANE,
             bytes_accessed=(8 + 4 * len(got)) * X * Z * ROWS * LANE,
             transcendentals=0,
         ),
-    )(core, grads, grads, *got)
+    )(core, grads, *got)
 
 
 def pack_kernel(owner_ref, parts_ref, params_ref, first_ref, second_ref, out_ref):

time: 81 us -> 80.8 us (level)
  no operation moved by 1% of the time
where the time goes in v5:
time: 80.8 us; the launch traced here: 80.1 us
  blocking collectives  69.9 us (87%)
  waiting for transfers between devices  3.38 us (4%)
  starting transfers between devices  2.18 us (3%)
  Pallas kernels  2 us (2%)
  local copies, waits for them, and re-layouts  1.9 us (2%)
    all_to_all x1, blocking collectives, body(): lax.all_to_all(chip.reshape(X * PAIR, FAR * ROWS, LANE), 'dp', 0, 0, axis...  31.3 us
    all_to_all x1, blocking collectives, body(): far = lax.all_to_all(near, 'dp', 0, 0, axis_index_groups=far_groups())  19.7 us
    all_to_all x1, blocking collectives, body(): handed = lax.all_to_all(packed, 'section', 0, 0)  18.8 us
    ppermute x1, waiting for transfers between devices, body(): got = lax.ppermute(sent, 'dp', swap)  3.38 us
    ppermute x1, starting transfers between devices, body(): got = lax.ppermute(sent, 'dp', swap)  2.18 us
    unnamed x12, local copies, waits for them, and re-layouts  1.9 us
  transfers between devices with their start and end apart: 1, of which 1 were waited for; matrix products, arithmetic and copies ran while one was open for 0% of the time, Pallas kernels for 0%

profile of v5, /device:TPU:6, one launch (start us, length us, event | category | flops | bytes accessed | tf_op | source)
XLA Modules:
  0.0 80.1 jit_solution(843230852411952225)
XLA Ops:
  0.6 0.0 copy-start
  0.7 1.9 %copy-done = bf16[1,2,1,6144,128]{4,3,2,1,0:T(8,128)(2,1)S(1)} copy-done((bf16[1,2,1,6144,128]{4,3,2,1,0:T(8,128)(2,1)S(1)}, bf16[1,2,1,6144,128]{4,3,2,1,0:T(8,128)(2,1)}, u32[]{:S(2)}) %copy-start) | copy-done | bytes 3145752
  2.5 0.0 copy-start.1
  2.5 0.2 shard_map.76
  2.7 2.2 %collective-permute-start = (f32[2,4,6,64,128]{4,3,2,1,0:T(8,128)S(1)}, f32[2,4,6,64,128]{4,3,2,1,0:T(8,128)S(1)}, u32[]{:S(2)}, u32[]{:S(2)}) collective-permute-start(f32[2,4,6,64,128]{4,3,2,1,0:T(8,128)S(1)} %shard_map.76), channel_id=1, source_target_pairs={{0,8},{8,0},{16,24},{24,16},{32,40},{40,32},{48,56},{56,48},{64,72... | collective-permute-start | bytes 4718600 | tf_op jit(solution)/shard_map/ppermute | solution.py:137
  4.9 3.4 %collective-permute-done.got_ref = f32[2,4,6,64,128]{4,3,2,1,0:T(8,128)S(1)} collective-permute-done((f32[2,4,6,64,128]{4,3,2,1,0:T(8,128)S(1)}, f32[2,4,6,64,128]{4,3,2,1,0:T(8,128)S(1)}, u32[]{:S(2)}, u32[]{:S(2)}) %collective-permute-start) | collective-permute-done | bytes 1572896 | tf_op jit(solution)/shard_map/ppermute | solution.py:137
  8.3 0.0 copy-done.1
  8.3 0.3 shard_map.77
  8.5 31.3 %all_to_all.15 = f32[8,384,128]{2,1,0:T(8,128)S(1)} all-to-all(f32[8,384,128]{2,1,0:T(8,128)S(1)} %bitcast.10), channel_id=1, replica_groups={{0,192,384,576,16,208,400,592},{8,200,392,584,24,216,408,600},{48,240,4..., dimensions={0} | all-to-all | bytes 3145728 | tf_op jit(solution)/shard_map/all_to_all | solution.py:139
  39.9 0.0 copy-start.2
  39.9 0.0 copy-start.3
  39.9 0.0 copy-start.4
  39.9 0.0 copy-start.5
  39.9 0.1 reduce_sum.9
  40.0 19.7 %all_to_all.16.parts_ref = f32[6,64,128]{2,1,0:T(8,128)S(1)} all-to-all(f32[6,64,128]{2,1,0:T(8,128)S(1)} %bitcast.15), channel_id=1, replica_groups={{0,48,64,112,128,176},{8,56,72,120,136,184},{16,32,80,96,144,160},{24,4..., dimensions={0} | all-to-all | bytes 393216 | tf_op jit(solution)/shard_map/all_to_all | solution.py:143
  59.7 0.0 copy-done.2
  59.7 0.0 copy-done.3
  59.7 0.0 copy-done.4
  59.7 0.0 copy-done.5
  59.7 0.6 shard_map.78
  60.3 18.8 %all_to_all.17.got_ref = f32[8,96,128]{2,1,0:T(8,128)S(1)} all-to-all(f32[8,96,128]{2,1,0:T(8,128)S(1)} %shard_map.78), channel_id=1, replica_groups=mesh['dp'=96,'section'=8] {'section'}, dimensions={0} | all-to-all | bytes 786432 | tf_op jit(solution)/shard_map/all_to_all | solution.py:151
  79.1 1.0 %shard_map.79 = (f32[1,256,128]{2,1,0:T(8,128)}, f32[1,256,128]{2,1,0:T(8,128)}, f32[1,256,128]{2,1,0:T(8,128)}) custom-call(f32[8,96,128]{2,1,0:T(8,128)S(1)} %all_to_all.17.got_ref), custom_call_target="tpu_custom_call" | custom-call | tf_op jit(solution)/shard_map/pallas_call | solution.py:153
Async XLA Ops:
  0.6 1.9 %copy-start = (bf16[1,2,1,6144,128]{4,3,2,1,0:T(8,128)(2,1)S(1)}, bf16[1,2,1,6144,128]{4,3,2,1,0:T(8,128)(2,1)}, u32[]{:S(2)}) copy-start(bf16[1,2,1,6144,128]{4,3,2,1,0:T(8,128)(2,1)} %param.5) | copy-start | bytes 9437188
  2.5 5.7 %copy-start.1 = (bf16[1,2,1,6144,128]{4,3,2,1,0:T(8,128)(2,1)S(1)}, bf16[1,2,1,6144,128]{4,3,2,1,0:T(8,128)(2,1)}, u32[]{:S(2)}) copy-start(bf16[1,2,1,6144,128]{4,3,2,1,0:T(8,128)(2,1)} %param.5) | copy-start | bytes 9437188
  2.7 5.6 %collective-permute-start = (f32[2,4,6,64,128]{4,3,2,1,0:T(8,128)S(1)}, f32[2,4,6,64,128]{4,3,2,1,0:T(8,128)S(1)}, u32[]{:S(2)}, u32[]{:S(2)}) collective-permute-start(f32[2,4,6,64,128]{4,3,2,1,0:T(8,128)S(1)} %shard_map.76), channel_id=1, source_target_pairs={{0,8},{8,0},{16,24},{24,16},{32,40},{40,32},{48,56},{56,48},{64,72... | collective-permute-start | bytes 4718600 | tf_op jit(solution)/shard_map/ppermute | solution.py:137
  39.9 19.8 %copy-start.2 = (f32[1,64,128]{2,1,0:T(8,128)S(1)}, f32[1,64,128]{2,1,0:T(8,128)}, u32[]{:S(2)}) copy-start(f32[1,64,128]{2,1,0:T(8,128)} %param.6) | copy-start | bytes 98308
  39.9 19.8 %copy-start.3 = (f32[1,64,128]{2,1,0:T(8,128)S(1)}, f32[1,64,128]{2,1,0:T(8,128)}, u32[]{:S(2)}) copy-start(f32[1,64,128]{2,1,0:T(8,128)} %param.7) | copy-start | bytes 98308
  39.9 19.8 %copy-start.4 = (f32[1,64,128]{2,1,0:T(8,128)S(1)}, f32[1,64,128]{2,1,0:T(8,128)}, u32[]{:S(2)}) copy-start(f32[1,64,128]{2,1,0:T(8,128)} %param.8) | copy-start | bytes 98308
  39.9 19.9 %copy-start.5 = (s32[1,1,8]{2,1,0:T(1,128)S(1)}, s32[1,1,8]{2,1,0:T(1,128)}, u32[]{:S(2)}) copy-start(s32[1,1,8]{2,1,0:T(1,128)} %param.9) | copy-start | bytes 100
